TPU v7x, 1024 devices: a whole 4x8x16 slice. The times are simulated.
1024 devices in a mesh: row: 32 (over x, y_lo, core), col: 32 (over z, y_hi).
Axes of the slice: x: 4, y: 8 (y_hi: 2, y_lo: 4; y = y_hi * 4 + y_lo), z: 16, core: 2. Of those that a mesh axis runs over, the one named last changes fastest.
Arguments:
- green: bfloat16 [4096, 57344], P('row', 'col'), may hold values from -0.0625 to 0.0625
- green_mask: int32 [32, 448], P('row', 'col'), may hold values 0 or 1
- tensor: bfloat16 [57344, 4096], P('row', 'col'), may hold values from -6 to 6
- tensor_mask: int32 [448, 32], P('row', 'col'), may hold values 0 or 1
Outputs:
- contracted: bfloat16 [4096, 4096], P('row', 'col')
All inputs are finite; a program needn't handle non-finite values. No bound on the sum of `green_mask` or of `tensor_mask` on one device may be relied on, other than what follows from the above.
Results may differ from a plain program's by a relative error of at most 0.001.
Values may be sent and summed in bfloat16 or wider, within the bound.
A program may use at most 32 MiB of HBM per device.

v0:
```python
import jax
import jax.numpy as jnp
from jax import lax
from jax.sharding import PartitionSpec as P

BLK = 128
WIN = 4


def shifted(value, axis, by):
    size = lax.axis_size(axis)
    return lax.ppermute(value, axis, [(i, (i + by) % size) for i in range(size)])


def widen(mask, size):
    return jnp.repeat(jnp.repeat(mask, size, axis=0), size, axis=1)


def shards(green, green_mask, tensor, tensor_mask):
    green_kept = green * widen(green_mask, BLK).astype(green.dtype)
    tensor_kept = tensor * widen(tensor_mask, BLK).astype(tensor.dtype)
    row_count = lax.axis_size("row")
    col_count = lax.axis_size("col")
    row_index = lax.axis_index("row")
    col_index = lax.axis_index("col")
    tile_width = tensor.shape[0]
    bit_count = col_count.bit_length() - 1
    bit_list = list(range(bit_count))
    green_base = green_kept
    tensor_base = tensor_kept
    for bit in bit_list:
        green_moved = shifted(green_base, "col", col_count - (1 << bit))
        green_base = jnp.where(row_index % col_count >> bit & 1 == 1, green_moved, green_base)
        tensor_moved = shifted(tensor_base, "row", row_count - (1 << bit))
        tensor_base = jnp.where(col_index >> bit & 1 == 1, tensor_moved, tensor_base)

    def pick(held, step):
        local = (row_index + col_index - step) % row_count // col_count
        return held

    total = jnp.dot(pick(green_base, 0), tensor_base, preferred_element_type=jnp.float32)
    green_now = green_base
    tensor_now = tensor_base
    for step in range(1, WIN):
        green_now = shifted(green_now, "col", 1)
        tensor_now = shifted(tensor_now, "row", 1)
        total = total + jnp.dot(
            pick(green_now, step), tensor_now, preferred_element_type=jnp.float32
        )
    return total.astype(jnp.bfloat16)


def solution(mesh):
    in_specs = (P("row", "col"), P("row", "col"), P("row", "col"), P("row", "col"))
    out_specs = P("row", "col")
    return jax.shard_map(shards, mesh=mesh, in_specs=in_specs, out_specs=out_specs, check_vma=False)
```

profile of v0, /device:TPU:98, one launch (start us, length us, event | category | flops | bytes accessed | tf_op | source)
XLA Modules:
  0.0 264.2 jit_solution(13594147469840289232)
XLA Ops:
  0.0 0.7 convert_bitcast_fusion.1
  0.7 1.1 broadcast_multiply_fusion.1
  1.9 2.0 collective-permute-start
  4.0 0.3 broadcast_multiply_fusion
  4.3 4.6 %collective-permute-start.5 = (bf16[1792,128]{1,0:T(8,128)(2,1)S(1)}, bf16[1792,128]{1,0:T(8,128)(2,1)S(1)}, u32[]{:S(2)}, u32[]{:S(2)}) collective-permute-start(bf16[1792,128]{1,0:T(8,128)(2,1)S(1)} %broadcast_multiply_fusion), channel_id=1, source_target_pairs={{0,992},{32,0},{64,32},{96,64},{128,96},{160,128},{192,160},{224,1... | collective-permute-start | bytes 1376264 | tf_op jit(solution)/shard_map/ppermute | solution.py:12
  9.0 21.3 %collective-permute-done = bf16[128,1792]{1,0:T(8,128)(2,1)S(1)} collective-permute-done((bf16[128,1792]{1,0:T(8,128)(2,1)S(1)}, bf16[128,1792]{1,0:T(8,128)(2,1)S(1)}, u32[]{:S(2)}, u32[]{:S(2)}) %collective-permute-start) | collective-permute-done | bytes 458784 | tf_op jit(solution)/shard_map/ppermute | solution.py:12
  30.4 1.9 collective-permute-start.1
  32.3 0.3 broadcast_select_fusion
  32.6 1.9 collective-permute-start.6
  34.5 8.3 %collective-permute-done.1 = bf16[128,1792]{1,0:T(8,128)(2,1)S(1)} collective-permute-done((bf16[128,1792]{1,0:T(8,128)(2,1)S(1)}, bf16[128,1792]{1,0:T(8,128)(2,1)S(1)}, u32[]{:S(2)}, u32[]{:S(2)}) %collective-permute-start.1) | collective-permute-done | bytes 458784 | tf_op jit(solution)/shard_map/ppermute | solution.py:12
  42.9 19.1 %collective-permute-start.2 = (bf16[128,1792]{1,0:T(8,128)(2,1)S(1)}, bf16[128,1792]{1,0:T(8,128)(2,1)S(1)}, u32[]{:S(2)}, u32[]{:S(2)}) collective-permute-start(bf16[128,1792]{1,0:T(8,128)(2,1)S(1)} %broadcast_select_fusion.6), channel_id=1, source_target_pairs={{0,28},{1,29},{2,30},{3,31},{4,0},{5,1},{6,2},{7,3},{8,4},{9,5},{1... | collective-permute-start | bytes 1376264 | tf_op jit(solution)/shard_map/ppermute | solution.py:12
  62.1 6.1 %collective-permute-start.7 = (bf16[1792,128]{1,0:T(8,128)(2,1)S(1)}, bf16[1792,128]{1,0:T(8,128)(2,1)S(1)}, u32[]{:S(2)}, u32[]{:S(2)}) collective-permute-start(bf16[1792,128]{1,0:T(8,128)(2,1)S(1)} %broadcast_select_fusion.1), channel_id=1, source_target_pairs={{0,896},{32,928},{64,960},{96,992},{128,0},{160,32},{192,64},{224,... | collective-permute-start | bytes 1376264 | tf_op jit(solution)/shard_map/ppermute | solution.py:12
  68.2 28.7 %collective-permute-done.2 = bf16[128,1792]{1,0:T(8,128)(2,1)S(1)} collective-permute-done((bf16[128,1792]{1,0:T(8,128)(2,1)S(1)}, bf16[128,1792]{1,0:T(8,128)(2,1)S(1)}, u32[]{:S(2)}, u32[]{:S(2)}) %collective-permute-start.2) | collective-permute-done | bytes 458784 | tf_op jit(solution)/shard_map/ppermute | solution.py:12
  96.9 1.9 collective-permute-start.3
  98.9 3.4 %collective-permute-start.8 = (bf16[1792,128]{1,0:T(8,128)(2,1)S(1)}, bf16[1792,128]{1,0:T(8,128)(2,1)S(1)}, u32[]{:S(2)}, u32[]{:S(2)}) collective-permute-start(bf16[1792,128]{1,0:T(8,128)(2,1)S(1)} %broadcast_select_fusion.2), channel_id=1, source_target_pairs={{0,768},{32,800},{64,832},{96,864},{128,896},{160,928},{192,960},{... | collective-permute-start | bytes 1376264 | tf_op jit(solution)/shard_map/ppermute | solution.py:12
  102.3 14.5 %collective-permute-done.3 = bf16[128,1792]{1,0:T(8,128)(2,1)S(1)} collective-permute-done((bf16[128,1792]{1,0:T(8,128)(2,1)S(1)}, bf16[128,1792]{1,0:T(8,128)(2,1)S(1)}, u32[]{:S(2)}, u32[]{:S(2)}) %collective-permute-start.3) | collective-permute-done | bytes 458784 | tf_op jit(solution)/shard_map/ppermute | solution.py:12
  116.9 10.9 %collective-permute-start.4 = (bf16[128,1792]{1,0:T(8,128)(2,1)S(1)}, bf16[128,1792]{1,0:T(8,128)(2,1)S(1)}, u32[]{:S(2)}, u32[]{:S(2)}) collective-permute-start(bf16[128,1792]{1,0:T(8,128)(2,1)S(1)} %broadcast_select_fusion.8), channel_id=1, source_target_pairs={{0,16},{1,17},{2,18},{3,19},{4,20},{5,21},{6,22},{7,23},{8,24},{9,... | collective-permute-start | bytes 1376264 | tf_op jit(solution)/shard_map/ppermute | solution.py:12
  127.9 3.0 %collective-permute-start.9 = (bf16[1792,128]{1,0:T(8,128)(2,1)S(1)}, bf16[1792,128]{1,0:T(8,128)(2,1)S(1)}, u32[]{:S(2)}, u32[]{:S(2)}) collective-permute-start(bf16[1792,128]{1,0:T(8,128)(2,1)S(1)} %broadcast_select_fusion.3), channel_id=1, source_target_pairs={{0,512},{32,544},{64,576},{96,608},{128,640},{160,672},{192,704},{... | collective-permute-start | bytes 1376264 | tf_op jit(solution)/shard_map/ppermute | solution.py:12
  130.9 36.9 %collective-permute-done.4 = bf16[128,1792]{1,0:T(8,128)(2,1)S(1)} collective-permute-done((bf16[128,1792]{1,0:T(8,128)(2,1)S(1)}, bf16[128,1792]{1,0:T(8,128)(2,1)S(1)}, u32[]{:S(2)}, u32[]{:S(2)}) %collective-permute-start.4) | collective-permute-done | bytes 458784 | tf_op jit(solution)/shard_map/ppermute | solution.py:12
  167.8 2.8 %collective-permute-start.10 = (bf16[128,1792]{1,0:T(8,128)(2,1)S(1)}, bf16[128,1792]{1,0:T(8,128)(2,1)S(1)}, u32[]{:S(2)}, u32[]{:S(2)}) collective-permute-start(bf16[128,1792]{1,0:T(8,128)(2,1)S(1)} %broadcast_select_fusion.9), channel_id=1, source_target_pairs={{0,1},{1,2},{2,3},{3,4},{4,5},{5,6},{6,7},{7,8},{8,9},{9,10},{10,1... | collective-permute-start | bytes 1376264 | tf_op jit(solution)/shard_map/ppermute | solution.py:12
  170.7 1.9 collective-permute-start.11
  172.7 24.4 %collective-permute-done.10 = bf16[128,1792]{1,0:T(8,128)(2,1)S(1)} collective-permute-done((bf16[128,1792]{1,0:T(8,128)(2,1)S(1)}, bf16[128,1792]{1,0:T(8,128)(2,1)S(1)}, u32[]{:S(2)}, u32[]{:S(2)}) %collective-permute-start.10) | collective-permute-done | bytes 458784 | tf_op jit(solution)/shard_map/ppermute | solution.py:12
  197.1 1.9 collective-permute-start.12
  199.0 17.1 %collective-permute-done.11 = bf16[1792,128]{1,0:T(8,128)(2,1)S(1)} collective-permute-done((bf16[1792,128]{1,0:T(8,128)(2,1)S(1)}, bf16[1792,128]{1,0:T(8,128)(2,1)S(1)}, u32[]{:S(2)}, u32[]{:S(2)}) %collective-permute-start.11) | collective-permute-done | bytes 458784 | tf_op jit(solution)/shard_map/ppermute | solution.py:12
  216.2 1.9 collective-permute-start.13
  218.1 0.3 fusion.1
  218.4 7.2 %collective-permute-done.12 = bf16[128,1792]{1,0:T(8,128)(2,1)S(1)} collective-permute-done((bf16[128,1792]{1,0:T(8,128)(2,1)S(1)}, bf16[128,1792]{1,0:T(8,128)(2,1)S(1)}, u32[]{:S(2)}, u32[]{:S(2)}) %collective-permute-start.12) | collective-permute-done | bytes 458784 | tf_op jit(solution)/shard_map/ppermute | solution.py:12
  225.6 1.9 collective-permute-start.14
  227.5 23.3 %collective-permute-done.13 = bf16[1792,128]{1,0:T(8,128)(2,1)S(1)} collective-permute-done((bf16[1792,128]{1,0:T(8,128)(2,1)S(1)}, bf16[1792,128]{1,0:T(8,128)(2,1)S(1)}, u32[]{:S(2)}, u32[]{:S(2)}) %collective-permute-start.13) | collective-permute-done | bytes 458784 | tf_op jit(solution)/shard_map/ppermute | solution.py:12
  250.8 1.9 collective-permute-start.15
  253.3 10.0 %collective-permute-done.15 = bf16[1792,128]{1,0:T(8,128)(2,1)S(1)} collective-permute-done((bf16[1792,128]{1,0:T(8,128)(2,1)S(1)}, bf16[1792,128]{1,0:T(8,128)(2,1)S(1)}, u32[]{:S(2)}, u32[]{:S(2)}) %collective-permute-start.15) | collective-permute-done | bytes 458784 | tf_op jit(solution)/shard_map/ppermute | solution.py:12
  263.3 0.9 fusion
  (26 shorter events, 1.2 us)
Async XLA Ops:
  0.7 3.1 %copy-start.2 = (s32[14,1]{0,1:T(1,128)S(1)}, s32[14,1]{0,1:T(1,128)}, u32[]{:S(2)}) copy-start(s32[14,1]{0,1:T(1,128)} %param.7) | copy-start | bytes 172
  0.7 3.2 %copy-start.1 = (bf16[1792,128]{1,0:T(8,128)(2,1)S(1)}, bf16[1792,128]{1,0:T(8,128)(2,1)}, u32[]{:S(2)}) copy-start(bf16[1792,128]{1,0:T(8,128)(2,1)} %param.6) | copy-start | bytes 1376260
  1.9 28.5 %collective-permute-start = (bf16[128,1792]{1,0:T(8,128)(2,1)S(1)}, bf16[128,1792]{1,0:T(8,128)(2,1)S(1)}, u32[]{:S(2)}, u32[]{:S(2)}) collective-permute-start(bf16[128,1792]{1,0:T(8,128)(2,1)S(1)} %broadcast_multiply_fusion.1), channel_id=1, source_target_pairs={{0,31},{1,0},{2,1},{3,2},{4,3},{5,4},{6,5},{7,6},{8,7},{9,8},{10,9... | collective-permute-start | bytes 1376264 | tf_op jit(solution)/shard_map/ppermute | solution.py:12
  4.0 26.3 %copy-start = (bf16[128,1792]{1,0:T(8,128)(2,1)S(1)}, bf16[128,1792]{1,0:T(8,128)(2,1)}, u32[]{:S(2)}) copy-start(bf16[128,1792]{1,0:T(8,128)(2,1)} %param.4) | copy-start | bytes 1376260
  4.3 28.0 %collective-permute-start.5 = (bf16[1792,128]{1,0:T(8,128)(2,1)S(1)}, bf16[1792,128]{1,0:T(8,128)(2,1)S(1)}, u32[]{:S(2)}, u32[]{:S(2)}) collective-permute-start(bf16[1792,128]{1,0:T(8,128)(2,1)S(1)} %broadcast_multiply_fusion), channel_id=1, source_target_pairs={{0,992},{32,0},{64,32},{96,64},{128,96},{160,128},{192,160},{224,1... | collective-permute-start | bytes 1376264 | tf_op jit(solution)/shard_map/ppermute | solution.py:12
  30.4 12.5 %collective-permute-start.1 = (bf16[128,1792]{1,0:T(8,128)(2,1)S(1)}, bf16[128,1792]{1,0:T(8,128)(2,1)S(1)}, u32[]{:S(2)}, u32[]{:S(2)}) collective-permute-start(bf16[128,1792]{1,0:T(8,128)(2,1)S(1)} %broadcast_select_fusion.5), channel_id=1, source_target_pairs={{0,30},{1,31},{2,0},{3,1},{4,2},{5,3},{6,4},{7,5},{8,6},{9,7},{10,... | collective-permute-start | bytes 1376264 | tf_op jit(solution)/shard_map/ppermute | solution.py:12
  32.6 29.4 %collective-permute-start.6 = (bf16[1792,128]{1,0:T(8,128)(2,1)S(1)}, bf16[1792,128]{1,0:T(8,128)(2,1)S(1)}, u32[]{:S(2)}, u32[]{:S(2)}) collective-permute-start(bf16[1792,128]{1,0:T(8,128)(2,1)S(1)} %broadcast_select_fusion), channel_id=1, source_target_pairs={{0,960},{32,992},{64,0},{96,32},{128,64},{160,96},{192,128},{224,1... | collective-permute-start | bytes 1376264 | tf_op jit(solution)/shard_map/ppermute | solution.py:12
  42.9 53.9 %collective-permute-start.2 = (bf16[128,1792]{1,0:T(8,128)(2,1)S(1)}, bf16[128,1792]{1,0:T(8,128)(2,1)S(1)}, u32[]{:S(2)}, u32[]{:S(2)}) collective-permute-start(bf16[128,1792]{1,0:T(8,128)(2,1)S(1)} %broadcast_select_fusion.6), channel_id=1, source_target_pairs={{0,28},{1,29},{2,30},{3,31},{4,0},{5,1},{6,2},{7,3},{8,4},{9,5},{1... | collective-permute-start | bytes 1376264 | tf_op jit(solution)/shard_map/ppermute | solution.py:12
  62.1 36.8 %collective-permute-start.7 = (bf16[1792,128]{1,0:T(8,128)(2,1)S(1)}, bf16[1792,128]{1,0:T(8,128)(2,1)S(1)}, u32[]{:S(2)}, u32[]{:S(2)}) collective-permute-start(bf16[1792,128]{1,0:T(8,128)(2,1)S(1)} %broadcast_select_fusion.1), channel_id=1, source_target_pairs={{0,896},{32,928},{64,960},{96,992},{128,0},{160,32},{192,64},{224,... | collective-permute-start | bytes 1376264 | tf_op jit(solution)/shard_map/ppermute | solution.py:12
  96.9 19.9 %collective-permute-start.3 = (bf16[128,1792]{1,0:T(8,128)(2,1)S(1)}, bf16[128,1792]{1,0:T(8,128)(2,1)S(1)}, u32[]{:S(2)}, u32[]{:S(2)}) collective-permute-start(bf16[128,1792]{1,0:T(8,128)(2,1)S(1)} %broadcast_select_fusion.7), channel_id=1, source_target_pairs={{0,24},{1,25},{2,26},{3,27},{4,28},{5,29},{6,30},{7,31},{8,0},{9,1... | collective-permute-start | bytes 1376264 | tf_op jit(solution)/shard_map/ppermute | solution.py:12
  98.9 28.9 %collective-permute-start.8 = (bf16[1792,128]{1,0:T(8,128)(2,1)S(1)}, bf16[1792,128]{1,0:T(8,128)(2,1)S(1)}, u32[]{:S(2)}, u32[]{:S(2)}) collective-permute-start(bf16[1792,128]{1,0:T(8,128)(2,1)S(1)} %broadcast_select_fusion.2), channel_id=1, source_target_pairs={{0,768},{32,800},{64,832},{96,864},{128,896},{160,928},{192,960},{... | collective-permute-start | bytes 1376264 | tf_op jit(solution)/shard_map/ppermute | solution.py:12
  116.9 50.9 %collective-permute-start.4 = (bf16[128,1792]{1,0:T(8,128)(2,1)S(1)}, bf16[128,1792]{1,0:T(8,128)(2,1)S(1)}, u32[]{:S(2)}, u32[]{:S(2)}) collective-permute-start(bf16[128,1792]{1,0:T(8,128)(2,1)S(1)} %broadcast_select_fusion.8), channel_id=1, source_target_pairs={{0,16},{1,17},{2,18},{3,19},{4,20},{5,21},{6,22},{7,23},{8,24},{9,... | collective-permute-start | bytes 1376264 | tf_op jit(solution)/shard_map/ppermute | solution.py:12
  127.9 42.8 %collective-permute-start.9 = (bf16[1792,128]{1,0:T(8,128)(2,1)S(1)}, bf16[1792,128]{1,0:T(8,128)(2,1)S(1)}, u32[]{:S(2)}, u32[]{:S(2)}) collective-permute-start(bf16[1792,128]{1,0:T(8,128)(2,1)S(1)} %broadcast_select_fusion.3), channel_id=1, source_target_pairs={{0,512},{32,544},{64,576},{96,608},{128,640},{160,672},{192,704},{... | collective-permute-start | bytes 1376264 | tf_op jit(solution)/shard_map/ppermute | solution.py:12
  167.8 29.3 %collective-permute-start.10 = (bf16[128,1792]{1,0:T(8,128)(2,1)S(1)}, bf16[128,1792]{1,0:T(8,128)(2,1)S(1)}, u32[]{:S(2)}, u32[]{:S(2)}) collective-permute-start(bf16[128,1792]{1,0:T(8,128)(2,1)S(1)} %broadcast_select_fusion.9), channel_id=1, source_target_pairs={{0,1},{1,2},{2,3},{3,4},{4,5},{5,6},{6,7},{7,8},{8,9},{9,10},{10,1... | collective-permute-start | bytes 1376264 | tf_op jit(solution)/shard_map/ppermute | solution.py:12
  170.7 45.4 %collective-permute-start.11 = (bf16[1792,128]{1,0:T(8,128)(2,1)S(1)}, bf16[1792,128]{1,0:T(8,128)(2,1)S(1)}, u32[]{:S(2)}, u32[]{:S(2)}) collective-permute-start(bf16[1792,128]{1,0:T(8,128)(2,1)S(1)} %broadcast_select_fusion.4), channel_id=1, source_target_pairs={{0,32},{32,64},{64,96},{96,128},{128,160},{160,192},{192,224},{224... | collective-permute-start | bytes 1376264 | tf_op jit(solution)/shard_map/ppermute | solution.py:12
  197.1 28.5 %collective-permute-start.12 = (bf16[128,1792]{1,0:T(8,128)(2,1)S(1)}, bf16[128,1792]{1,0:T(8,128)(2,1)S(1)}, u32[]{:S(2)}, u32[]{:S(2)}) collective-permute-start(bf16[128,1792]{1,0:T(8,128)(2,1)S(1)} %collective-permute-done.10), channel_id=1, source_target_pairs={{0,1},{1,2},{2,3},{3,4},{4,5},{5,6},{6,7},{7,8},{8,9},{9,10},{10,1... | collective-permute-start | bytes 1376264 | tf_op jit(solution)/shard_map/ppermute | solution.py:12
  216.2 34.6 %collective-permute-start.13 = (bf16[1792,128]{1,0:T(8,128)(2,1)S(1)}, bf16[1792,128]{1,0:T(8,128)(2,1)S(1)}, u32[]{:S(2)}, u32[]{:S(2)}) collective-permute-start(bf16[1792,128]{1,0:T(8,128)(2,1)S(1)} %collective-permute-done.11), channel_id=1, source_target_pairs={{0,32},{32,64},{64,96},{96,128},{128,160},{160,192},{192,224},{224... | collective-permute-start | bytes 1376264 | tf_op jit(solution)/shard_map/ppermute | solution.py:12
  225.6 27.7 %collective-permute-start.14 = (bf16[128,1792]{1,0:T(8,128)(2,1)S(1)}, bf16[128,1792]{1,0:T(8,128)(2,1)S(1)}, u32[]{:S(2)}, u32[]{:S(2)}) collective-permute-start(bf16[128,1792]{1,0:T(8,128)(2,1)S(1)} %collective-permute-done.12), channel_id=1, source_target_pairs={{0,1},{1,2},{2,3},{3,4},{4,5},{5,6},{6,7},{7,8},{8,9},{9,10},{10,1... | collective-permute-start | bytes 1376264 | tf_op jit(solution)/shard_map/ppermute | solution.py:12
  250.8 12.5 %collective-permute-start.15 = (bf16[1792,128]{1,0:T(8,128)(2,1)S(1)}, bf16[1792,128]{1,0:T(8,128)(2,1)S(1)}, u32[]{:S(2)}, u32[]{:S(2)}) collective-permute-start(bf16[1792,128]{1,0:T(8,128)(2,1)S(1)} %collective-permute-done.13), channel_id=1, source_target_pairs={{0,32},{32,64},{64,96},{96,128},{128,160},{160,192},{192,224},{224... | collective-permute-start | bytes 1376264 | tf_op jit(solution)/shard_map/ppermute | solution.py:12
where the time goes:
time: 265 us; the launch traced here: 264 us
  waiting for transfers between devices  192 us (72%)
  starting transfers between devices  67.2 us (25%)
  other arithmetic  2.83 us (1%)
    ppermute x16, waiting for transfers between devices, shifted(): lax.ppermute(value, axis, [(i, (i + by) % size) for i in range(size)])  192 us
    ppermute x16, starting transfers between devices, shifted(): lax.ppermute(value, axis, [(i, (i + by) % size) for i in range(size)])  67.2 us
  transfers between devices with their start and end apart: 16, of which 10 were waited for; matrix products, arithmetic and copies ran while one was open for 1% of the time, Pallas kernels for 0%

commit v1 on v0

v1 whole, which is shorter than its diff:
```python
import jax
import jax.numpy as jnp
from jax import lax
from jax.experimental import pallas as pl
from jax.experimental.pallas import tpu as pltpu
from jax.sharding import PartitionSpec as P

MESH = pl.DeviceIdType.MESH
BLK = 128
WHOLE = ((0, 1, 2), (4, 5, 6), (7, 8, 9), (11, 12, 13))
SHARED = (3, 3, 10, 10)
ROWS_FROM = (0, 64, 64, 0)
GP = 448
BP = 512
HALF = GP // 2
HOPS = 10


def kernel(green, gmask, tensor, tmask, out, gpart, bpart, z0, z1, z2a, z2b, z3, bx, by, acc, got, other,
           gx_send, gx_recv, bx_send, bx_recv, z_send, z_recv, y_send, y_recv, c_send, o_send, o_recv, h_send, h_recv):
    row, col = lax.axis_index("row"), lax.axis_index("col")
    x, low, core = row // 8, (row // 2) % 4, row % 2
    z, half = col // 2, col % 2
    y = 4 * half + low
    down = ((core - half) + 1) // 2
    up = ((half - core) + 1) // 2
    odd = down + up

    def at(x, y, z, core):
        return ((x * 4 + y % 4) * 2 + core, z * 2 + y // 4)

    z_up, z_down = at(x, y, (z + 1) % 16, core), at(x, y, (z + 15) % 16, core)
    mate = at(x, y, z, 1 - core)
    barrier = pltpu.get_barrier_semaphore()
    friends = [at((x + d) % 4, y, z, core) for d in (1, 2, 3)]
    friends += [at(x, (y + d) % 8, z, core) for d in range(1, 8)]
    friends += [z_up, z_down, mate]
    for friend in friends:
        pl.semaphore_signal(barrier, inc=1, device_id=friend, device_id_type=MESH)

    def kept_green(b, first, count):
        scale = gmask[0, b].astype(jnp.float32)
        return (green[pl.ds(first, count), b * BLK:(b + 1) * BLK].astype(jnp.float32) * scale).astype(jnp.bfloat16)

    def kept_tensor(b):
        scale = tmask[b, 0].astype(jnp.float32)
        return (tensor[b * BLK:(b + 1) * BLK, :].astype(jnp.float32) * scale).astype(jnp.bfloat16)

    for q in range(4):
        for n, b in enumerate(WHOLE[q]):
            gpart[q, n * BLK:(n + 1) * BLK, :] = kept_green(b, 0, BLK)
        gpart[q, 3 * BLK:GP, :] = kept_green(SHARED[q], ROWS_FROM[q], 64)
    for q in range(4):
        for n, b in enumerate(WHOLE[q] + (SHARED[q],)):
            bpart[q, n * BLK:(n + 1) * BLK, :] = kept_tensor(b)

    pl.semaphore_wait(barrier, len(friends))

    def remote(src, dst, send, recv, device):
        return pltpu.make_async_remote_copy(src_ref=src, dst_ref=dst, send_sem=send, recv_sem=recv,
                                            device_id=device, device_id_type=MESH)

    lands = (
        ((z0.at[4], 0, GP, 0),),
        ((z1.at[0], 0, GP, 1),),
        ((z2a.at[0], 0, HALF, 2), (z2b.at[0], HALF, HALF, 3)),
        ((z3.at[0], 0, GP, 4),),
    )
    for p in range(4):
        @pl.when(x == p)
        def _():
            for d in (2, 1, 3):
                q = (p + d) % 4
                for dst, first, count, s in lands[p]:
                    remote(gpart.at[q, pl.ds(first, count)], dst, gx_send.at[d, s], gx_recv.at[s], at(q, y, z, core)).start()
            for dst, first, count, s in lands[p]:
                pltpu.make_async_copy(gpart.at[p, pl.ds(first, count)], dst, gx_recv.at[s]).start()
    pltpu.make_async_copy(bpart.at[x], bx.at[x], bx_recv.at[x]).start()
    for d in (2, 1, 3):
        q = (x + d) % 4
        remote(bpart.at[q], bx.at[x], bx_send.at[d], bx_recv.at[x], at(q, y, z, core)).start()

    far_down = jnp.where(low < 2, 1, 0)
    n2b = 9 - low + up
    n2a = jnp.where(low < 2, 8 + low + down, n2b)
    n0d, n0u = low + down, jnp.maximum(1 + up - low, 0)
    n1, n3 = low + 4 + down, 5 - low + up

    def step(number, hops, slot, device, t):
        @pl.when(jnp.logical_and(t >= 1, t <= hops))
        def _():
            remote(slot(t), slot(t), z_send.at[number, t], z_recv.at[number, t], device).wait_recv()

        @pl.when(t < hops)
        def _():
            remote(slot(t), slot(t + 1), z_send.at[number, t + 1], z_recv.at[number, t + 1], device).start()

    a_row = (x * 4 + low) * 2 + core
    a_device = (a_row, jnp.where(low < 2, (z + 15) % 16, (z + 1) % 16) * 2 + half)
    conveyors = (
        (0, n2a, lambda t: z2a.at[t], a_device),
        (1, n2b, lambda t: z2b.at[t], z_up),
        (2, n1, lambda t: z1.at[t], z_down),
        (3, n3, lambda t: z3.at[t], z_up),
        (4, n0d, lambda t: z0.at[4 - t], z_down),
        (5, n0u, lambda t: z0.at[4 + t], z_up),
    )
    for p in range(4):
        for dst, first, count, s in lands[p]:
            pltpu.make_async_copy(dst, dst, gx_recv.at[s]).wait()
    for conveyor in conveyors:
        step(*conveyor, 0)

    for p in range(4):
        pltpu.make_async_copy(bx.at[p], bx.at[p], bx_recv.at[p]).wait()

    def target(e):
        return 4 * core + (low - z + e + 16) % 4

    def send_y(e):
        device_y = target(e)

        @pl.when(device_y == y)
        def _():
            pltpu.make_async_copy(bx, by.at[half, e + 1], y_recv.at[half, e + 1]).start()

        @pl.when(device_y != y)
        def _():
            remote(bx, by.at[half, e + 1], y_send.at[e + 1], y_recv.at[half, e + 1], at(x, device_y, z, core)).start()

    def sent_y(e):
        device_y = target(e)

        @pl.when(device_y != y)
        def _():
            remote(bx, by.at[half, e + 1], y_send.at[e + 1], y_recv.at[half, e + 1], at(x, device_y, z, core)).wait_send()

    extra = 3 * core - 1
    send_y(0)
    send_y(1)

    @pl.when(odd == 1)
    def _():
        send_y(extra)

    def later(t, carry):
        for conveyor in conveyors:
            step(*conveyor, t)
        return carry

    lax.fori_loop(1, HOPS + 1, later, 0)

    def have(hj, e):
        pltpu.make_async_copy(bx, by.at[hj, e + 1], y_recv.at[hj, e + 1]).wait()

    def hand(hj, e):
        return remote(by.at[hj, e + 1], by.at[hj, e + 1], c_send.at[hj, e + 1], y_recv.at[hj, e + 1], mate)

    for h in range(2):
        pieces = ((1, 0), (0, 1), (1, 1), (0, 2)) if h else ((1, -1), (0, 0), (1, 0), (0, 1))
        alone = (0, 0) if h else (1, 1)

        @pl.when(jnp.logical_and(half == h, core == h))
        def _():
            for piece in pieces:
                have(*piece)
                hand(*piece).start()
            have(*alone)

        @pl.when(jnp.logical_and(half == h, core != h))
        def _():
            for piece in pieces:
                have(*piece)

    acc[...] = jnp.zeros_like(acc)
    shared_rows = 64 * ((x * (3 - x)) // 2)
    for n in range(3):
        e = n - down

        def products():
            for p in range(4):
                if p == 0:
                    part = z0[4 - low + e]
                elif p == 1:
                    part = z1[4 + low - e]
                elif p == 2:
                    hop = 8 - low + e
                    part = jnp.concatenate([z2a[jnp.where(low < 2, 8 + low - e, hop)], z2b[hop]], axis=0)
                else:
                    part = z3[4 - low + e]
                wide = jnp.concatenate([part[:BLK], part[BLK:2 * BLK], part[2 * BLK:3 * BLK]], axis=1)
                rest = part[3 * BLK:]
                place = ((low + 4 * p + z - e + 16) % 16) // 4
                for hj in range(2):
                    s = core + hj - half + 2 * e

                    @pl.when(jnp.logical_and(s >= 0, s <= 3))
                    def _():
                        block = by[hj, e + 1, place, :3 * BLK]
                        last = by[hj, e + 1, place, 3 * BLK:]
                        acc[p, hj] += jnp.dot(wide, block, preferred_element_type=jnp.float32)
                        acc[p, hj, pl.ds(pl.multiple_of(shared_rows, 64), 64)] += jnp.dot(
                            rest, last, preferred_element_type=jnp.float32)

        if n < 2:
            products()
        else:
            pl.when(odd == 1)(products)

    def give(d):
        q = (x + d) % 4
        return remote(acc.at[q], got.at[x], o_send.at[d], o_recv.at[x], at(q, y, z, core))

    for d in (2, 1, 3):
        give(d).start()
    for d in (1, 3, 2):
        p = (x + d) % 4
        pltpu.make_async_copy(got.at[p], got.at[p], o_recv.at[p]).wait()
        acc[x] += got[p]
    swap = remote(acc.at[x, 1 - half], other, h_send, h_recv, at(x, (y + 4) % 8, z, core))
    swap.start()
    swap.wait_recv()
    out[...] = (acc[x, half] + other[...]).astype(jnp.bfloat16)

    swap.wait_send()
    for d in (1, 2, 3):
        give(d).wait_send()
        remote(bpart.at[x], bx.at[x], bx_send.at[d], bx_recv.at[x], mate).wait_send()
    for p in range(4):
        @pl.when(x == p)
        def _():
            for d in (1, 2, 3):
                for dst, first, count, s in lands[p]:
                    remote(gpart.at[p, pl.ds(first, count)], dst, gx_send.at[d, s], gx_recv.at[s], mate).wait_send()
    sent_y(0)
    sent_y(1)

    @pl.when(odd == 1)
    def _():
        sent_y(extra)

    for h in range(2):
        pieces = ((1, 0), (0, 1), (1, 1), (0, 2)) if h else ((1, -1), (0, 0), (1, 0), (0, 1))

        @pl.when(jnp.logical_and(half == h, core == h))
        def _():
            for piece in pieces:
                hand(*piece).wait_send()

    def drain(t, carry):
        for number, hops, slot, device in conveyors:
            @pl.when(t < hops)
            def _():
                remote(slot(t), slot(t + 1), z_send.at[number, t + 1], z_recv.at[number, t + 1], device).wait_send()
        return carry

    lax.fori_loop(0, HOPS, drain, 0)


def shards(green, green_mask, tensor, tensor_mask):
    vmem, smem = pl.BlockSpec(memory_space=pltpu.VMEM), pl.BlockSpec(memory_space=pltpu.SMEM)
    half, single, dma = jnp.bfloat16, jnp.float32, pltpu.SemaphoreType.DMA
    return pl.pallas_call(
        kernel,
        name="window",
        out_shape=jax.ShapeDtypeStruct((BLK, BLK), half),
        in_specs=[vmem, smem, vmem, smem],
        out_specs=vmem,
        scratch_shapes=[
            pltpu.VMEM((4, GP, BLK), half), pltpu.VMEM((4, BP, BLK), half),
            pltpu.VMEM((7, GP, BLK), half), pltpu.VMEM((9, GP, BLK), half),
            pltpu.VMEM((HOPS + 1, HALF, BLK), half), pltpu.VMEM((HOPS + 1, HALF, BLK), half),
            pltpu.VMEM((7, GP, BLK), half),
            pltpu.VMEM((4, BP, BLK), half), pltpu.VMEM((2, 4, 4, BP, BLK), half),
            pltpu.VMEM((4, 2, BLK, BLK), single), pltpu.VMEM((4, 2, BLK, BLK), single), pltpu.VMEM((BLK, BLK), single),
            dma((4, 5)), dma((5,)), dma((4,)), dma((4,)), dma((6, HOPS + 1)), dma((6, HOPS + 1)),
            dma((4,)), dma((2, 4)), dma((2, 4)), dma((4,)), dma((4,)), dma, dma,
        ],
        compiler_params=pltpu.CompilerParams(collective_id=0, has_side_effects=True, vmem_limit_bytes=40 << 20),
        cost_estimate=pl.CostEstimate(flops=8 * BLK * BLK * 1792, bytes_accessed=2 * 2 * BLK * 1792, transcendentals=0),
    )(green, green_mask, tensor, tensor_mask)


def solution(mesh):
    spec = P("row", "col")
    return jax.shard_map(shards, mesh=mesh, in_specs=(spec,) * 4, out_specs=spec, check_vma=False)
```

time: 265 us -> 93.3 us (0.35)
  the two profiles are of different devices: /device:TPU:98 before, /device:TPU:16 now
where the time goes in v1:
time: 93.3 us; the launch traced here: 92.7 us
  Pallas kernels  89.3 us (96%)
  local copies, waits for them, and re-layouts  3.41 us (4%)
    pallas_call x1, Pallas kernels, shards(): pl.pallas_call(kernel, name='window', out_shape=jax.ShapeDtypeStruct((BLK...  89.3 us
    unnamed x8, local copies, waits for them, and re-layouts  3.41 us

profile of v1, /device:TPU:16, one launch (start us, length us, event | category | flops | bytes accessed | tf_op | source)
XLA Modules:
  0.0 92.7 jit_solution(2476958207553818540)
XLA Ops:
  0.0 0.0 copy-start.2
  0.0 0.8 copy.5.tmask
  0.8 0.0 copy-done.2
  0.8 0.0 copy-start
  0.8 1.0 %copy-done = bf16[128,1792]{1,0:T(8,128)(2,1)S(1)} copy-done((bf16[128,1792]{1,0:T(8,128)(2,1)S(1)}, bf16[128,1792]{1,0:T(8,128)(2,1)}, u32[]{:S(2)}) %copy-start) | copy-done | bytes 458776
  1.8 0.0 copy-start.1
  1.8 1.0 %copy-done.1 = bf16[1792,128]{1,0:T(8,128)(2,1)S(1)} copy-done((bf16[1792,128]{1,0:T(8,128)(2,1)S(1)}, bf16[1792,128]{1,0:T(8,128)(2,1)}, u32[]{:S(2)}) %copy-start.1) | copy-done | bytes 458776
  2.8 89.3 %window.1 = bf16[128,128]{1,0:T(8,128)(2,1)S(1)} custom-call(bf16[128,1792]{1,0:T(8,128)(2,1)S(1)} %copy-done, s32[1,14]{1,0:T(1,128)S(1)} %copy-done.2, bf16[1792,128]{1,0:T(8,128)(2,1)S(1)} %copy-done.1, s32[14,1]{1,0:T(8,128)S(1)} %copy.5.tmask), custom_call_target="tpu_custom_call" | custom-call | flops 234881024 | bytes 917504 | tf_op jit(solution)/shard_map/window/pallas_call | solution.py:263
  92.1 0.6 copy.7
Async XLA Ops:
  0.0 0.8 copy-start.2
  0.8 1.0 %copy-start = (bf16[128,1792]{1,0:T(8,128)(2,1)S(1)}, bf16[128,1792]{1,0:T(8,128)(2,1)}, u32[]{:S(2)}) copy-start(bf16[128,1792]{1,0:T(8,128)(2,1)} %green.1) | copy-start | bytes 1376260
  1.8 1.0 %copy-start.1 = (bf16[1792,128]{1,0:T(8,128)(2,1)S(1)}, bf16[1792,128]{1,0:T(8,128)(2,1)}, u32[]{:S(2)}) copy-start(bf16[1792,128]{1,0:T(8,128)(2,1)} %tensor.1) | copy-start | bytes 1376260

commit v2 on v0

v2 whole, which is shorter than its diff:
```python
import jax
import jax.numpy as jnp
from jax import lax
from jax.experimental import pallas as pl
from jax.experimental.pallas import tpu as pltpu
from jax.sharding import PartitionSpec as P

MESH = pl.DeviceIdType.MESH
BLK = 128
SUB = 64
WIDTH = 14 * BLK
WHOLE = ((0, 1, 2), (4, 5, 6), (7, 8, 9), (11, 12, 13))
SHARED = (3, 3, 10, 10)
LAST = (0, 1, 0, 1)
PART = 3 * BLK + SUB
CUTS = ((0, 112), (112, 224), (336, 112))
Z_HOPS = 10
Y_HOPS = 5
ORDER = (0, 1, 3, 2)
HOP_CODES = (
    (
        ((0x828049, 0x940049), (0x920003, 0x228003), (0x740013, 0x920013), (0x880052, 0x740052)),
        ((0x144600, 0x024600), (0x014248, 0xb44248), (0x02b488, 0x014488), (0x124680, 0x02b680)),
    ),
    (
        ((0x800a49, 0x880a49), (0x900000, 0x968003), (0x6c0013, 0x920013), (0x880052, 0x758052)),
        ((0x16c000, 0x124000), (0x02c24d, 0x004248), (0x0eb488, 0x014488), (0x124680, 0x01b680)),
    ),
)


def kernel(green_hbm, gmask, tensor_hbm, tmask, out, green, tensor, gpart, bpart, z0, z1, z2a, z2b, z2c, z3, by, acc, got,
           in_sem, gx_send, gx_recv, bx_send, z_send, z_recv, y_send, y_recv, c_send, c_recv, o_send, o_recv):
    row, col = lax.axis_index("row"), lax.axis_index("col")
    x, low, core = row // 8, (row // 2) % 4, row % 2
    z, half = col // 2, col % 2
    y = 4 * half + low
    down = ((core - half) + 1) // 2
    up = ((half - core) + 1) // 2
    odd = down + up

    def at(x, y, z, core):
        return ((x * 4 + y % 4) * 2 + core, z * 2 + y // 4)

    def remote(src, dst, send, recv, device):
        return pltpu.make_async_remote_copy(src_ref=src, dst_ref=dst, send_sem=send, recv_sem=recv,
                                            device_id=device, device_id_type=MESH)

    z_up, z_down = at(x, y, (z + 1) % 16, core), at(x, y, (z + 15) % 16, core)
    def picked(*cases):
        chosen = 0
        for case_low, case_half in cases:
            chosen = chosen + jnp.where(jnp.logical_and(low == case_low, half == case_half), 1, 0)
        return chosen

    a_down = picked((0, 1), (1, 0))
    b_down = picked((0, 0), (0, 1), (1, 1))
    far_up, far_down = 9 - low + up, 8 + low + down
    n0d, n0u = low + down, jnp.maximum(1 + up - low, 0)
    n1, n3 = low + 4 + down, 5 - low + up

    mate = at(x, y, z, 1 - core)
    load_green = pltpu.make_async_copy(green_hbm, green, in_sem.at[0])
    load_tensor = pltpu.make_async_copy(tensor_hbm, tensor, in_sem.at[1])
    load_green.start()
    load_tensor.start()
    barrier = pltpu.get_barrier_semaphore()
    friends = [at((x + d) % 4, y, z, core) for d in (1, 2, 3)]
    friends += [at((x + d) % 4, (y + 4) % 8, z, core) for d in (1, 2, 3)]
    friends += [at(x, (y + d) % 8, z, core) for d in range(1, 8)]
    friends += [at(x, y, (z - way * jnp.maximum(hops - 1 - odd, 1) + 16) % 16, core) for hops, way in (
        (jnp.where(b_down == 1, far_down, far_up), 1 - 2 * b_down), (jnp.where(a_down == 1, far_down, far_up), 1 - 2 * a_down),
        (far_up, 1), (n1, -1), (n3, 1), (n0d, -1))]
    friends += [z_up, z_down, mate]
    for friend in friends:
        pl.semaphore_signal(barrier, inc=1, device_id=friend, device_id_type=MESH)

    load_tensor.wait()
    for q in range(4):
        for n, b in enumerate(WHOLE[q]):
            scale = tmask[b, 0].astype(jnp.float32)
            block = tensor[b * BLK:(b + 1) * BLK, :].astype(jnp.float32)
            bpart[q, n * BLK:(n + 1) * BLK, :] = (block * scale).astype(jnp.bfloat16)
        b = SHARED[q]
        first = b * BLK + SUB * LAST[q]
        block = tensor[first:first + SUB, :].astype(jnp.float32) * tmask[b, 0].astype(jnp.float32)
        bpart[q, 3 * BLK:, :] = block.astype(jnp.bfloat16)
    pl.semaphore_wait(barrier, len(friends))
    pltpu.make_async_copy(bpart.at[x], by.at[y, x], y_recv.at[y, x]).start()
    for d in (2, 1, 3):
        q = (x + d) % 4
        remote(bpart.at[q], by.at[y, x], bx_send.at[d], y_recv.at[y, x], at(q, y, z, core)).start()


    load_green.wait()
    left = lax.broadcasted_iota(jnp.int32, (SUB, BLK), 1) < SUB
    for q in range(4):
        for n, b in enumerate(WHOLE[q]):
            scale = gmask[0, b].astype(jnp.float32)
            block = green[:, b * BLK:(b + 1) * BLK].astype(jnp.float32)
            gpart[q, n * BLK:(n + 1) * BLK, :] = (block * scale).astype(jnp.bfloat16)
        b = SHARED[q]
        block = green[:, b * BLK:(b + 1) * BLK].astype(jnp.float32) * gmask[0, b].astype(jnp.float32)
        top, bottom = block[:SUB], block[SUB:]
        if LAST[q]:
            both = jnp.where(left, pltpu.roll(top, SUB, 1), bottom)
        else:
            both = jnp.where(left, top, pltpu.roll(bottom, SUB, 1))
        gpart[q, 3 * BLK:, :] = both.astype(jnp.bfloat16)

    lands = (
        ((z0.at[4], 0, PART, 0),),
        ((z1.at[0], 0, PART, 1),),
        tuple((ref.at[0], *cut, 2 + n) for n, (ref, cut) in enumerate(zip((z2a, z2b, z2c), CUTS))),
        ((z3.at[0], 0, PART, 5),),
    )
    for p in range(4):
        @pl.when(x == p)
        def _():
            for dst, first, count, s in lands[p]:
                pltpu.make_async_copy(gpart.at[p, pl.ds(first, count)], dst, gx_recv.at[s]).start()
            for d in (2, 1, 3):
                q = (p + d) % 4
                for dst, first, count, s in lands[p]:
                    remote(gpart.at[q, pl.ds(first, count)], dst, gx_send.at[d, s], gx_recv.at[s], at(q, y, z, core)).start()

    conveyors = (
        (1, 2, jnp.where(b_down == 1, far_down, far_up), lambda t: z2b.at[t], 1 - 2 * b_down),
        (0, 2, jnp.where(a_down == 1, far_down, far_up), lambda t: z2a.at[t], 1 - 2 * a_down),
        (2, 2, far_up, lambda t: z2c.at[t], 1),
        (3, 1, n1, lambda t: z1.at[t], -1),
        (4, 3, n3, lambda t: z3.at[t], 1),
        (5, 0, n0d, lambda t: z0.at[4 - t], -1),
        (6, 0, n0u, lambda t: z0.at[4 + t], 1),
    )

    def jump_of(hops):
        return jnp.maximum(hops - 1 - odd, 0)

    def hop(number, slot, way, t, by_hops):
        device = at(x, y, (z + way * by_hops + 16) % 16, core)
        return remote(slot(t), slot(t + by_hops), z_send.at[number, t + by_hops], z_recv.at[number, t + by_hops], device)

    def z_first(p):
        for dst, first, count, s in lands[p]:
            pltpu.make_async_copy(dst, dst, gx_recv.at[s]).wait()
        for number, part, hops, slot, way in conveyors:
            if part == p:
                @pl.when(hops > 0)
                def _():
                    hop(number, slot, way, 0, jnp.maximum(jump_of(hops), 1)).start()

    def z_step(step, parts):
        for number, part, hops, slot, way in conveyors:
            t = jump_of(hops) + step
            if part in parts:
                @pl.when(jnp.logical_and(t > 0, t <= hops))
                def _():
                    hop(number, slot, way, t - 1, 1).wait_recv()

                    @pl.when(t < hops)
                    def _():
                        hop(number, slot, way, t, 1).start()

    def codes_of(pair, way):
        code = 0
        for m in range(4):
            for c in range(2):
                here = jnp.logical_and(z % 4 == m, core == c)
                code = code + jnp.where(here, HOP_CODES[pair][way][m][c], 0)
        return code

    codes = tuple(tuple(codes_of(pair, way) for way in range(2)) for pair in range(2))

    def y_hops(pair, way, o):
        return lax.shift_right_logical(codes[pair][way], 3 * ((o + 4 * core) % 8)) % 8

    def wanted(way, o, t):
        origin = (o + 4 * core) % 8
        place = (origin + (t if way == 0 else 8 - t)) % 8
        e = (place - origin + z + 16) % 4
        third = jnp.logical_and(origin >= 4, e == 3 - core)
        return jnp.logical_and(place < 4, jnp.logical_or(e < 2, third))

    def y_hop(way, t, o, p, hops):
        by_hops = hops - t
        for d in (4, 3, 2, 1):
            by_hops = jnp.where(jnp.logical_and(t + d <= hops, wanted(way, o, t + d)), d, by_hops)
        device = at(x, (y + (by_hops if way == 0 else 8 - by_hops)) % 8, z, core)
        return remote(by.at[o, p], by.at[o, p], y_send.at[way, t, p], y_recv.at[o, p], device)

    e_mate = (2 * half - 1 - 1) // 2

    def piece_of(o):
        return 2 * ((low + z - e_mate - o % 4 + 16) % 4) + o // 4 - 1

    def hand(o, p):
        piece = piece_of(o)
        return remote(by.at[o, p], by.at[8 + piece, p], c_send.at[o, p], c_recv.at[piece, p], mate)

    def handed(o):
        piece = piece_of(o)
        return jnp.logical_and(core == half, jnp.logical_and(piece >= 0, piece <= 3))

    def y_step(a, t):
        p = (x + ORDER[a]) % 4

        def arrived(o):
            pltpu.make_async_copy(by.at[o, p], by.at[o, p], y_recv.at[o, p]).wait()

        @pl.when(t == 0)
        def _():
            arrived(y)
            for way in range(2):
                hops = y_hops(a // 2, way, y)

                @pl.when(hops > 0)
                def _():
                    y_hop(way, 0, y, p, hops).start()

            @pl.when(jnp.logical_and(handed(y), half == core))
            def _():
                hand(y, p).start()

        @pl.when(jnp.logical_and(t > 0, t <= Y_HOPS))
        def _():
            for way in range(2):
                o = (y + (8 - t if way == 0 else t)) % 8
                hops = y_hops(a // 2, way, o)

                @pl.when(jnp.logical_and(hops >= t, wanted(way, o, t)))
                def _():
                    arrived(o)

                    @pl.when(hops > t)
                    def _():
                        y_hop(way, t, o, p, hops).start()

                    @pl.when(handed(o))
                    def _():
                        hand(o, p).start()

    y_step(0, 0)
    for p in range(4):
        pl.when(x == p)(lambda p=p: z_first(p))

    def y_all(t, carry):
        for a in range(4):
            y_step(a, t - a)

        @pl.when(t == 2)
        def _():
            for p in range(4):
                pl.when(x != p)(lambda p=p: z_first(p))

        @pl.when(t == 5)
        def _():
            z_step(0, (0, 3))

        @pl.when(t == 6)
        def _():
            z_step(0, (1,))
            z_step(1, (0, 3))

        @pl.when(t == 7)
        def _():
            z_step(0, (2,))
            z_step(1, (1,))
            z_step(2, (0, 3))

        return carry

    lax.fori_loop(1, Y_HOPS + 4, y_all, 0)

    @pl.when(odd == 1)
    def _():
        for piece in range(4):
            for p in range(4):
                pltpu.make_async_copy(by.at[8 + piece, p], by.at[8 + piece, p], c_recv.at[piece, p]).wait()

    acc[...] = jnp.zeros_like(acc)
    nothing = jnp.zeros((SUB, BLK), jnp.bfloat16)

    def one(p, n):
        e = n - down
        if p == 0:
            part = z0[4 - low + e]
        elif p == 1:
            part = z1[4 + low - e]
        elif p == 2:
            h_up, h_down = 8 - low + e, 8 + low - e
            part = jnp.concatenate([z2a[jnp.where(a_down == 1, h_down, h_up)], z2b[jnp.where(b_down == 1, h_down, h_up)],
                                    z2c[h_up]], axis=0)
        else:
            part = z3[4 - low + e]
        wide = jnp.concatenate([part[:BLK], part[BLK:2 * BLK], part[2 * BLK:3 * BLK]], axis=1)
        rest = part[3 * BLK:]
        place = ((low + 4 * p + z - e + 16) % 16) // 4
        for hj in range(2):
            s = core + hj - half + 2 * e

            @pl.when(jnp.logical_and(s >= 0, s <= 3))
            def _():
                where = jnp.where(odd == 1, 8 + 2 * n + hj - 1, 4 * hj + (low + z - e + 16) % 4)
                other = by[where, place]
                last = other[3 * BLK:]
                ends = jnp.concatenate([jnp.concatenate([last, nothing], axis=0), jnp.concatenate([nothing, last], axis=0)], axis=1)
                total = jnp.dot(wide, other[:3 * BLK], preferred_element_type=jnp.float32)
                pair = jnp.dot(rest, ends, preferred_element_type=jnp.float32)
                acc[p, hj] += total + jnp.concatenate([pair[:, :BLK], pair[:, BLK:]], axis=0)

    def give(p, hj):
        return remote(acc.at[p, hj], got.at[2 * x + hj], o_send.at[p, hj], o_recv.at[2 * x + hj], at(p, y, z, core))

    def give_last(hj):
        return remote(acc.at[2, hj], got.at[2 * x + half], o_send.at[2, hj], o_recv.at[2 * x + half], at(2, 4 * hj + low, z, core))

    swap = remote(acc.at[x, 1 - half], got.at[8], o_send.at[x, half], o_recv.at[8], at(x, (y + 4) % 8, z, core))

    def took(n):
        pltpu.make_async_copy(got.at[n], got.at[n], o_recv.at[n]).wait()

    def products(p):
        one(p, 0)
        one(p, 1)

        @pl.when(odd == 1)
        def _():
            one(p, 2)

        for hj in range(2):
            if p == 2:
                @pl.when(jnp.logical_or(x != 2, half != hj))
                def _():
                    give_last(hj).start()
            else:
                @pl.when(x != p)
                def _():
                    give(p, hj).start()

    def sum_x():
        for d in (1, 3, 2):
            for hj in range(2):
                n = 2 * ((x + d) % 4) + hj
                took(n)
                acc[x, hj] += got[n]
        swap.start()

    products(0)
    products(3)
    z_step(1, (2,))
    z_step(2, (1,))
    products(1)
    z_step(2, (2,))
    products(2)
    pl.when(x != 2)(sum_x)

    @pl.when(x != 2)
    def _():
        took(8)
        out[...] = (acc[x, half] + got[8]).astype(jnp.bfloat16)

    @pl.when(x == 2)
    def _():
        total = acc[2, half]
        for d in range(1, 8):
            n = (4 + half + d) % 8
            took(n)
            total = total + got[n]
        out[...] = total.astype(jnp.bfloat16)

    for p in range(4):
        for hj in range(2):
            if p == 2:
                @pl.when(jnp.logical_or(x != 2, half != hj))
                def _():
                    give_last(hj).wait_send()
            else:
                @pl.when(x != p)
                def _():
                    give(p, hj).wait_send()

        @pl.when(x == p)
        def _():
            for d in (1, 2, 3):
                for dst, first, count, s in lands[p]:
                    remote(gpart.at[p, pl.ds(first, count)], dst, gx_send.at[d, s], gx_recv.at[s], mate).wait_send()
    for d in (1, 2, 3):
        remote(bpart.at[x], by.at[y, x], bx_send.at[d], y_recv.at[y, x], mate).wait_send()

    pl.when(x != 2)(swap.wait_send)
    for number, part, hops, slot, way in conveyors:
        jump = jump_of(hops)

        @pl.when(hops > 0)
        def _():
            hop(number, slot, way, 0, jnp.maximum(jump, 1)).wait_send()

        for step in range(3):
            t = jump + step

            @pl.when(jnp.logical_and(t > 0, t < hops))
            def _():
                hop(number, slot, way, t, 1).wait_send()

    def drain(t, carry):
        for a in range(4):
            p = (x + ORDER[a]) % 4
            for way in range(2):
                o = (y + (8 - t if way == 0 else t)) % 8
                hops = y_hops(a // 2, way, o)

                @pl.when(jnp.logical_and(hops > t, jnp.logical_or(t == 0, wanted(way, o, t))))
                def _():
                    y_hop(way, t, o, p, hops).wait_send()

                reached = hops >= t if way == 0 else jnp.logical_and(hops >= t, t > 0)

                @pl.when(jnp.logical_and(handed(o), reached))
                def _():
                    hand(o, p).wait_send()
        return carry

    lax.fori_loop(0, Y_HOPS + 1, drain, 0)


def shards(green, green_mask, tensor, tensor_mask):
    vmem, smem, hbm = (pl.BlockSpec(memory_space=space) for space in (pltpu.VMEM, pltpu.SMEM, pltpu.HBM))
    half, single, dma = jnp.bfloat16, jnp.float32, pltpu.SemaphoreType.DMA
    slots = Z_HOPS + 1
    return pl.pallas_call(
        kernel,
        name="window",
        out_shape=jax.ShapeDtypeStruct((BLK, BLK), half),
        in_specs=[hbm, smem, hbm, smem],
        out_specs=vmem,
        scratch_shapes=[
            pltpu.VMEM((BLK, WIDTH), half), pltpu.VMEM((WIDTH, BLK), half),
            pltpu.VMEM((4, PART, BLK), half), pltpu.VMEM((4, PART, BLK), half),
            pltpu.VMEM((7, PART, BLK), half), pltpu.VMEM((9, PART, BLK), half),
            *(pltpu.VMEM((slots, count, BLK), half) for _, count in CUTS),
            pltpu.VMEM((7, PART, BLK), half), pltpu.VMEM((12, 4, PART, BLK), half),
            pltpu.VMEM((4, 2, BLK, BLK), single), pltpu.VMEM((9, BLK, BLK), single),
            dma((2,)), dma((4, 6)), dma((6,)), dma((4,)), dma((7, slots)), dma((7, slots)),
            dma((2, Y_HOPS + 1, 4)), dma((8, 4)), dma((8, 4)), dma((4, 4)), dma((4, 2)), dma((9,)),
        ],
        compiler_params=pltpu.CompilerParams(collective_id=0, has_side_effects=True, vmem_limit_bytes=60 << 20),
        cost_estimate=pl.CostEstimate(flops=8 * BLK * BLK * WIDTH, bytes_accessed=4 * BLK * WIDTH, transcendentals=0),
    )(green, green_mask, tensor, tensor_mask)


def solution(mesh):
    spec = P("row", "col")
    return jax.shard_map(shards, mesh=mesh, in_specs=(spec,) * 4, out_specs=spec, check_vma=False)
```

time: 265 us -> 84 us (0.32)
  the two profiles are of different devices: /device:TPU:98 before, /device:TPU:16 now
where the time goes in v2:
time: 84 us; the launch traced here: 83.7 us
  Pallas kernels  81 us (96%)
  local copies, waits for them, and re-layouts  2.71 us (3%)
    pallas_call x1, Pallas kernels, shards(): pl.pallas_call(kernel, name='window', out_shape=jax.ShapeDtypeStruct((BLK...  81 us
    unnamed x2, local copies, waits for them, and re-layouts  2.71 us

profile of v2, /device:TPU:16, one launch (start us, length us, event | category | flops | bytes accessed | tf_op | source)
XLA Modules:
  0.0 83.7 jit_solution(8182916674384530664)
XLA Ops:
  0.0 1.3 %copy.5.tmask = s32[14,1]{1,0:T(8,128)} copy(s32[14,1]{0,1:T(1,128)} %param.7) | data formatting | bytes 112 | tf_op args[3]
  1.3 81.0 %window.1 = bf16[128,128]{1,0:T(8,128)(2,1)} custom-call(bf16[128,1792]{1,0:T(8,128)(2,1)} %green_hbm.1, s32[1,14]{1,0:T(1,128)} %gmask.1, bf16[1792,128]{1,0:T(8,128)(2,1)} %tensor_hbm.1, s32[14,1]{1,0:T(8,128)} %copy.5.tmask), custom_call_target="tpu_custom_call" | custom-call | flops 234881024 | bytes 917504 | tf_op jit(solution)/shard_map/window/pallas_call | solution.py:431
  82.4 1.4 %copy.7 = bf16[128,128]{1,0:T(8,128)(2,1)} copy(bf16[128,128]{1,0:T(8,128)(2,1)} %window.1) | data formatting | bytes 65536

commit v3 on v2

--- a/solution.py
+++ b/solution.py
@@ -17,6 +17,7 @@
 Z_HOPS = 10
 Y_HOPS = 5
 ORDER = (0, 1, 3, 2)
+DIRECT = (1, 2)
 HOP_CODES = (
     (
         ((0x828049, 0x940049), (0x920003, 0x228003), (0x740013, 0x920013), (0x880052, 0x740052)),
@@ -53,7 +54,7 @@
             chosen = chosen + jnp.where(jnp.logical_and(low == case_low, half == case_half), 1, 0)
         return chosen
 
-    a_down = picked((0, 1), (1, 0))
+    a_down = picked((0, 1), (1, 0)) + (1 - core) * picked((2, 1))
     b_down = picked((0, 0), (0, 1), (1, 1))
     far_up, far_down = 9 - low + up, 8 + low + down
     n0d, n0u = low + down, jnp.maximum(1 + up - low, 0)
@@ -75,15 +76,17 @@
     for friend in friends:
         pl.semaphore_signal(barrier, inc=1, device_id=friend, device_id_type=MESH)
 
+    acc[...] = jnp.zeros_like(acc)
+
     load_tensor.wait()
     for q in range(4):
         for n, b in enumerate(WHOLE[q]):
-            scale = tmask[b, 0].astype(jnp.float32)
+            scale = tmask[0, b].astype(jnp.float32)
             block = tensor[b * BLK:(b + 1) * BLK, :].astype(jnp.float32)
             bpart[q, n * BLK:(n + 1) * BLK, :] = (block * scale).astype(jnp.bfloat16)
         b = SHARED[q]
         first = b * BLK + SUB * LAST[q]
-        block = tensor[first:first + SUB, :].astype(jnp.float32) * tmask[b, 0].astype(jnp.float32)
+        block = tensor[first:first + SUB, :].astype(jnp.float32) * tmask[0, b].astype(jnp.float32)
         bpart[q, 3 * BLK:, :] = block.astype(jnp.bfloat16)
     pl.semaphore_wait(barrier, len(friends))
     pltpu.make_async_copy(bpart.at[x], by.at[y, x], y_recv.at[y, x]).start()
@@ -278,7 +281,6 @@
             for p in range(4):
                 pltpu.make_async_copy(by.at[8 + piece, p], by.at[8 + piece, p], c_recv.at[piece, p]).wait()
 
-    acc[...] = jnp.zeros_like(acc)
     nothing = jnp.zeros((SUB, BLK), jnp.bfloat16)
 
     def one(p, n):
@@ -312,8 +314,12 @@
     def give(p, hj):
         return remote(acc.at[p, hj], got.at[2 * x + hj], o_send.at[p, hj], o_recv.at[2 * x + hj], at(p, y, z, core))
 
-    def give_last(hj):
-        return remote(acc.at[2, hj], got.at[2 * x + half], o_send.at[2, hj], o_recv.at[2 * x + half], at(2, 4 * hj + low, z, core))
+    def give_owner(p, hj):
+        return remote(acc.at[p, hj], got.at[2 * x + half], o_send.at[p, hj], o_recv.at[2 * x + half], at(p, 4 * hj + low, z, core))
+
+    direct = x < 0
+    for p in DIRECT:
+        direct = jnp.logical_or(direct, x == p)
 
     swap = remote(acc.at[x, 1 - half], got.at[8], o_send.at[x, half], o_recv.at[8], at(x, (y + 4) % 8, z, core))
 
@@ -329,10 +335,10 @@
             one(p, 2)
 
         for hj in range(2):
-            if p == 2:
-                @pl.when(jnp.logical_or(x != 2, half != hj))
-                def _():
-                    give_last(hj).start()
+            if p in DIRECT:
+                @pl.when(jnp.logical_or(x != p, half != hj))
+                def _():
+                    give_owner(p, hj).start()
             else:
                 @pl.when(x != p)
                 def _():
@@ -353,28 +359,28 @@
     products(1)
     z_step(2, (2,))
     products(2)
-    pl.when(x != 2)(sum_x)
-
-    @pl.when(x != 2)
+    pl.when(jnp.logical_not(direct))(sum_x)
+
+    @pl.when(jnp.logical_not(direct))
     def _():
         took(8)
         out[...] = (acc[x, half] + got[8]).astype(jnp.bfloat16)
 
-    @pl.when(x == 2)
+    @pl.when(direct)
     def _():
-        total = acc[2, half]
+        total = acc[x, half]
         for d in range(1, 8):
-            n = (4 + half + d) % 8
+            n = (2 * x + half + d) % 8
             took(n)
             total = total + got[n]
         out[...] = total.astype(jnp.bfloat16)
 
     for p in range(4):
         for hj in range(2):
-            if p == 2:
-                @pl.when(jnp.logical_or(x != 2, half != hj))
-                def _():
-                    give_last(hj).wait_send()
+            if p in DIRECT:
+                @pl.when(jnp.logical_or(x != p, half != hj))
+                def _():
+                    give_owner(p, hj).wait_send()
             else:
                 @pl.when(x != p)
                 def _():
@@ -388,7 +394,7 @@
     for d in (1, 2, 3):
         remote(bpart.at[x], by.at[y, x], bx_send.at[d], y_recv.at[y, x], mate).wait_send()
 
-    pl.when(x != 2)(swap.wait_send)
+    pl.when(jnp.logical_not(direct))(swap.wait_send)
     for number, part, hops, slot, way in conveyors:
         jump = jump_of(hops)
 
@@ -446,7 +452,7 @@
         ],
         compiler_params=pltpu.CompilerParams(collective_id=0, has_side_effects=True, vmem_limit_bytes=60 << 20),
         cost_estimate=pl.CostEstimate(flops=8 * BLK * BLK * WIDTH, bytes_accessed=4 * BLK * WIDTH, transcendentals=0),
-    )(green, green_mask, tensor, tensor_mask)
+    )(green, green_mask, tensor, tensor_mask.T)
 
 
 def solution(mesh):

time: 84 us -> 82.8 us (0.986)
  the two profiles are of different devices: /device:TPU:16 before, /device:TPU:1 now
where the time goes in v3:
time: 82.8 us; the launch traced here: 82.6 us
  Pallas kernels  81.2 us (98%)
  local copies, waits for them, and re-layouts  1.38 us (2%)
    pallas_call x1, Pallas kernels, shards(): pl.pallas_call(kernel, name='window', out_shape=jax.ShapeDtypeStruct((BLK...  81.2 us

profile of v3, /device:TPU:1, one launch (start us, length us, event | category | flops | bytes accessed | tf_op | source)
XLA Modules:
  0.0 82.6 jit_solution(13049144370948658263)
XLA Ops:
  0.0 81.2 %window.1 = bf16[128,128]{1,0:T(8,128)(2,1)} custom-call(bf16[128,1792]{1,0:T(8,128)(2,1)} %green_hbm.1, s32[1,14]{1,0:T(1,128)} %gmask.1, bf16[1792,128]{1,0:T(8,128)(2,1)} %tensor_hbm.1, s32[1,14]{1,0:T(1,128)} %bitcast.1), custom_call_target="tpu_custom_call" | custom-call | flops 234881024 | bytes 917504 | tf_op jit(solution)/shard_map/window/pallas_call | solution.py:437
  81.2 1.4 %copy.6 = bf16[128,128]{1,0:T(8,128)(2,1)} copy(bf16[128,128]{1,0:T(8,128)(2,1)} %window.1) | data formatting | bytes 65536
